TPU v7x, 32 devices: a whole 2x2x4 slice. The times are simulated.
32 devices in a mesh: rows: 4 (over y, x), cols: 8 (over z, core).
Axes of the slice: x: 2, y: 2, z: 4, core: 2. Of those that a mesh axis runs over, the one named last changes fastest.
Arguments:
- velocity: float32 [4, 512, 16384], P(None, 'rows', 'cols'), may hold values from -6 to 6
- layer_gap: float32 [512, 16384], P('rows', 'cols'), may hold values from -6 to 6
- surface: float32 [512, 16384], P('rows', 'cols'), may hold values from -3 to 3
- basin_depth: float32 [512, 16384], P('rows', 'cols'), may hold values from 0.25 to 1
- ocean_mask: int32 [512, 16384], P('rows', 'cols'), may hold values 0 or 1
Outputs:
- predicted: float32 [4, 512, 16384], P(None, 'rows', 'cols')
- new_surface: float32 [512, 16384], P('rows', 'cols')
All inputs are finite; a program needn't handle non-finite values. No bound on the sum of `ocean_mask` on one device may be relied on, other than what follows from the above.
Results may differ from a plain program's by a relative error of at most 0.0003.
Values sent between devices are 32-bit elements; how exact they have to be, the bound alone decides.
A program may use at most 128 MiB of HBM per device.

v0:
```python
import math

import jax
import jax.numpy as jnp
from jax import lax
from jax.sharding import PartitionSpec as P

NX = 16384
ITERS = 3
REACH = 4096


coriolis_dt = 0.1
viscous_dt = 0.05
buoyant_dt = 0.2
top_share = 0.3
transport_dt = 0.5
cross_weight = 0.5


def carried_in(part, axis, combine, identity, reverse):
    count = lax.axis_size(axis)
    place = lax.axis_index(axis)
    ahead = count - 1 - place if reverse else place
    gathered = jax.tree.map(lambda a: lax.all_gather(a, axis), part)
    state = jax.tree.map(lambda a, e: jnp.zeros_like(a) + jnp.asarray(e, a.dtype), part, identity)

    def one(hop, state):
        source = count - 1 - hop if reverse else hop
        return combine(
            state, jax.tree.map(lambda a: lax.dynamic_index_in_dim(a, source, 0, False), gathered)
        )

    return lax.fori_loop(0, ahead, one, state)


def extended(block, sides, width):
    for axis, dim in sides:
        count = lax.axis_size(axis)
        forward = [(i, i + 1) for i in range(count - 1)]
        backward = [(target, source) for source, target in forward]
        low = lax.ppermute(
            lax.slice_in_dim(block, block.shape[dim] - width, None, axis=dim), axis, forward
        )
        high = lax.ppermute(lax.slice_in_dim(block, 0, width, axis=dim), axis, backward)
        block = jnp.concatenate([low, block, high], axis=dim)
    return block


def neighbour(padded, rim_width, margin, row_step, column_step):
    height = padded.shape[-2] - 2 * rim_width + 2 * margin
    breadth = padded.shape[-1] - 2 * rim_width + 2 * margin
    top_row = rim_width - margin + row_step
    left_column = rim_width - margin + column_step
    return padded[..., top_row : top_row + height, left_column : left_column + breadth]


def predict(padded, rim_width, margin):
    velocity = padded[:4]
    centre = neighbour(velocity, rim_width, margin, 0, 0)
    spread = (
        neighbour(velocity, rim_width, margin, 0, 1)
        + neighbour(velocity, rim_width, margin, 0, -1)
        + neighbour(velocity, rim_width, margin, 1, 0)
        + neighbour(velocity, rim_width, margin, -1, 0)
        - 4.0 * centre
    )
    layer_gap = padded[4]
    slope_east = 0.5 * (
        neighbour(layer_gap, rim_width, margin, 0, 1)
        - neighbour(layer_gap, rim_width, margin, 0, -1)
    )
    slope_north = 0.5 * (
        neighbour(layer_gap, rim_width, margin, 1, 0)
        - neighbour(layer_gap, rim_width, margin, -1, 0)
    )
    upper_east = centre[0] + coriolis_dt * centre[1] + viscous_dt * spread[0]
    upper_north = centre[1] - coriolis_dt * centre[0] + viscous_dt * spread[1]
    lower_east = (
        centre[2] + coriolis_dt * centre[3] - buoyant_dt * slope_east + viscous_dt * spread[2]
    )
    lower_north = (
        centre[3] - coriolis_dt * centre[2] - buoyant_dt * slope_north + viscous_dt * spread[3]
    )
    return jnp.stack([upper_east, upper_north, lower_east, lower_north])


def transports(predicted, column_depth):
    flux_east = column_depth * (top_share * predicted[0] + (1.0 - top_share) * predicted[2])
    flux_north = column_depth * (top_share * predicted[1] + (1.0 - top_share) * predicted[3])
    return jnp.stack([flux_east, flux_north])


def divergence(padded_flux):
    return 0.5 * (
        neighbour(padded_flux[0], 1, 0, 0, 1) - neighbour(padded_flux[0], 1, 0, 0, -1)
    ) + 0.5 * (neighbour(padded_flux[1], 1, 0, 1, 0) - neighbour(padded_flux[1], 1, 0, -1, 0))


def operate(padded_surface, padded_depth, stiffness):
    centre = neighbour(padded_surface, 1, 0, 0, 0)
    depth_here = neighbour(padded_depth, 1, 0, 0, 0)
    result = centre
    for row_step, column_step, weight in (
        (0, 1, stiffness),
        (0, -1, stiffness),
        (1, 0, cross_weight),
        (-1, 0, cross_weight),
    ):
        conductance = jnp.sqrt(depth_here * neighbour(padded_depth, 1, 0, row_step, column_step))
        result = result + weight * conductance * (
            centre - neighbour(padded_surface, 1, 0, row_step, column_step)
        )
    return result


def line_constants():
    diagonal_base = 1.0 + 2.0 * cross_weight
    stiffness = diagonal_base * REACH**2
    root_term = math.sqrt(diagonal_base * diagonal_base + 4.0 * diagonal_base * stiffness)
    decay_lag = (diagonal_base + root_term) / (diagonal_base + 2.0 * stiffness + root_term)
    log_ratio = math.log(1.0 - decay_lag)
    centre_gain = 1.0 / (diagonal_base + 2.0 * stiffness * decay_lag)
    return (stiffness, log_ratio, centre_gain)


def sweeps(values, log_ratio):
    line_count, length = values.shape
    block_size = min(128, length)
    blocks = length // block_size
    pieces = values.reshape(line_count, blocks, block_size)
    offsets = jnp.arange(block_size)
    distance = offsets[None, :] - offsets[:, None]
    within = jnp.where(distance >= 0, jnp.exp(distance.astype(jnp.float32) * log_ratio), 0.0)
    onward = jnp.einsum("cbj,ji->cbi", pieces, within, precision=lax.Precision.HIGHEST)
    backward_part = jnp.einsum("cbj,ij->cbi", pieces, within, precision=lax.Precision.HIGHEST)
    block_ids = jnp.arange(blocks)
    block_gap = block_ids[None, :] - block_ids[:, None] - 1
    carry_table = jnp.where(
        block_gap >= 0, jnp.exp(block_gap.astype(jnp.float32) * (block_size * log_ratio)), 0.0
    )
    block_ends = onward[:, :, block_size - 1]
    starts = backward_part[:, :, 0]
    from_left = jnp.einsum("cs,sb->cb", block_ends, carry_table, precision=lax.Precision.HIGHEST)
    from_right = jnp.einsum("cs,bs->cb", starts, carry_table, precision=lax.Precision.HIGHEST)
    rising = jnp.exp((offsets + 1).astype(jnp.float32) * log_ratio)
    falling = jnp.exp((block_size - offsets).astype(jnp.float32) * log_ratio)
    onward = onward + from_left[:, :, None] * rising
    backward_part = backward_part + from_right[:, :, None] * falling
    return (onward.reshape(line_count, length), backward_part.reshape(line_count, length))


def assemble(values, onward, backward_part, line_first, line_last, start, log_ratio, centre_gain):
    position = (start + jnp.arange(values.shape[1])).astype(jnp.float32)
    line_length = float(NX)
    left_images = jnp.exp((position + 1.0) * log_ratio) + jnp.exp(
        (2.0 * line_length - position) * log_ratio
    )
    right_images = jnp.exp((line_length - position) * log_ratio) + jnp.exp(
        (line_length + 1.0 + position) * log_ratio
    )
    return centre_gain * (
        onward
        + backward_part
        - values
        + left_images * line_first[:, None]
        + right_images * line_last[:, None]
    )


def carry_link(earlier, later):
    return (earlier[0] * later[1] + later[0], earlier[1] * later[1])


def line_solve(residual, log_ratio, centre_gain):
    length = residual.shape[1]
    onward, backward_part = sweeps(residual, log_ratio)
    hop_decay = math.exp(length * log_ratio)
    local_ends = onward[:, -1]
    local_starts = backward_part[:, 0]
    hop_factor = jnp.full_like(local_ends, hop_decay)
    zero_carry = (jnp.zeros_like(local_ends), jnp.ones_like(local_ends))
    from_west = carried_in((local_ends, hop_factor), "cols", carry_link, zero_carry, False)[0]
    from_east = carried_in((local_starts, hop_factor), "cols", carry_link, zero_carry, True)[0]
    offsets = jnp.arange(length).astype(jnp.float32)
    onward = onward + from_west[:, None] * jnp.exp((offsets + 1.0) * log_ratio)
    backward_part = backward_part + from_east[:, None] * jnp.exp((length - offsets) * log_ratio)
    column_index = lax.axis_index("cols")
    device_count = lax.axis_size("cols")
    west_weight = jnp.exp(column_index.astype(jnp.float32) * (length * log_ratio))
    east_weight = jnp.exp(
        (device_count - 1 - column_index).astype(jnp.float32) * (length * log_ratio)
    )
    line_first, line_last = lax.psum((local_starts * west_weight, local_ends * east_weight), "cols")
    return assemble(
        residual,
        onward,
        backward_part,
        line_first,
        line_last,
        column_index * length,
        log_ratio,
        centre_gain,
    )


def per_device(velocity, layer_gap, surface, basin_depth, ocean_mask):
    wet_cells = ocean_mask.astype(jnp.float32)
    wet_depth = basin_depth * wet_cells
    stiffness, log_ratio, centre_gain = line_constants()
    state_stack = jnp.concatenate([velocity, layer_gap[None], wet_depth[None]], axis=0)
    padded = extended(state_stack, (("rows", 1), ("cols", 2)), 1)
    predicted = predict(padded, 1, 0) * wet_cells
    padded_flux = extended(transports(predicted, wet_depth), (("rows", 1), ("cols", 2)), 1)
    padded_depth = padded[5]
    forcing = wet_cells * (surface - transport_dt * divergence(padded_flux))
    surface_level = jnp.zeros_like(surface)
    residual = forcing
    for iteration in range(ITERS):
        surface_level = surface_level + wet_cells * line_solve(residual, log_ratio, centre_gain)
        if iteration + 1 < ITERS:
            padded_level = extended(surface_level, (("rows", 0), ("cols", 1)), 1)
            residual = wet_cells * (forcing - operate(padded_level, padded_depth, stiffness))
    return (predicted, math.sqrt(REACH) * surface_level)


def solution(mesh):
    placed = (
        P(None, "rows", "cols"),
        P("rows", "cols"),
        P("rows", "cols"),
        P("rows", "cols"),
        P("rows", "cols"),
    )
    return jax.shard_map(
        per_device,
        mesh=mesh,
        in_specs=placed,
        out_specs=(P(None, "rows", "cols"), P("rows", "cols")),
        check_vma=False,
    )
```

profile of v0, /device:TPU:0, one launch (start us, length us, event | category | flops | bytes accessed | tf_op | source)
XLA Modules:
  0.0 284.5 jit_solution(15162529295630734293)
XLA Ops:
  3.6 4.8 %collective-permute-start = (f32[6,1,2048]{2,1,0:T(1,128)S(1)}, f32[6,1,2048]{2,1,0:T(1,128)S(1)}, u32[]{:S(2)}, u32[]{:S(2)}) collective-permute-start(f32[6,1,2048]{2,1,0:T(1,128)S(1)} %get-tuple-element.514), channel_id=1, source_target_pairs={{0,8},{8,16},{16,24},{1,9},{9,17},{17,25},{2,10},{10,18},{18,26},{... | collective-permute-start | bytes 147464 | tf_op jit(solution)/shard_map/ppermute | solution.py:42
  10.2 4.3 %collective-permute-done.1 = f32[6,1,2048]{2,1,0:T(1,128)S(1)} collective-permute-done((f32[6,1,2048]{2,1,0:T(1,128)S(1)}, f32[6,1,2048]{2,1,0:T(1,128)S(1)}, u32[]{:S(2)}, u32[]{:S(2)}) %collective-permute-start.1) | collective-permute-done | bytes 49184 | tf_op jit(solution)/shard_map/ppermute | solution.py:45
  14.4 2.9 %pad_maximum_fusion = f32[6,130,2048]{2,1,0:T(8,128)S(1)} fusion(f32[6,1,2048]{2,1,0:T(1,128)S(1)} %collective-permute-done.1, f32[1,128,2048]{2,1,0:T(8,128)S(1)} %fusion.187, f32[1,128,2048]{2,1,0:T(8,128)S(1)} %bitcast.171, f32[4,128,2048]{2,1,0:T(8,128)} %param.17, f32[6,1,2048]{2,1,0:T(1,128)S(1)} %collective-permute-done), kind=kLoop, calls=%fused_computation.6 | loop fusion | flops 6389760 | bytes 12779520 | tf_op jit(solution)/shard_map/concatenate | solution.py:46
  17.3 2.8 copy-done.2
  21.6 3.1 %collective-permute-start.3 = (f32[6,130,1]{2,1,0:T(8,128)S(1)}, f32[6,130,1]{2,1,0:T(8,128)S(1)}, u32[]{:S(2)}, u32[]{:S(2)}) collective-permute-start(f32[6,130,1]{2,1,0:T(8,128)S(1)} %get-tuple-element.510), channel_id=1, source_target_pairs={{0,1},{1,2},{2,3},{3,4},{4,5},{5,6},{6,7},{8,9},{9,10},{10,11},{11... | collective-permute-start | bytes 9368 | tf_op jit(solution)/shard_map/ppermute | solution.py:42
  27.3 9.1 %concatenate.65 = f32[6,130,2050]{2,1,0:T(8,128)} concatenate(f32[6,130,1]{2,1,0:T(8,128)S(1)} %collective-permute-done.3, f32[6,130,2048]{2,1,0:T(8,128)} %copy-done.2, f32[6,130,1]{2,1,0:T(8,128)S(1)} %collective-permute-done.2), dimensions={2} | concatenate | bytes 12792000 | tf_op jit(solution)/shard_map/concatenate | solution.py:46
  39.4 12.0 %fusion.1 = f32[4,128,2048]{2,1,0:T(8,128)S(1)} fusion(f32[6,1,2048]{2,1,0:T(1,128)S(1)} %collective-permute-done, f32[1,128,2048]{2,1,0:T(8,128)S(1)} %fusion.187, f32[1,128,2048]{2,1,0:T(8,128)} %bitcast.170, f32[4,128,2048]{2,1,0:T(8,128)S(1)} %copy-done.1, f32[6,1,2048]{2,1,0:T(1,128)S(1)} %collective-permute-done.1, f32[6,130,1]{2,1,0:T(8,128)} %copy-done.21, ...), kind=kLoop, calls=%fused_computation.9 | loop fusion | flops 22020096 | bytes 10590304 | tf_op jit(solution)/shard_map/sub | solution.py:62
  56.4 4.3 %collective-permute-start.4 = (f32[2,1,2048]{2,1,0:T(1,128)S(1)}, f32[2,1,2048]{2,1,0:T(1,128)S(1)}, u32[]{:S(2)}, u32[]{:S(2)}) collective-permute-start(f32[2,1,2048]{2,1,0:T(1,128)S(1)} %get-tuple-element.519), channel_id=1, source_target_pairs={{0,8},{8,16},{16,24},{1,9},{9,17},{17,25},{2,10},{10,18},{18,26},{... | collective-permute-start | bytes 49160 | tf_op jit(solution)/shard_map/ppermute | solution.py:42
  62.1 4.3 %collective-permute-done.5 = f32[2,1,2048]{2,1,0:T(1,128)S(1)} collective-permute-done((f32[2,1,2048]{2,1,0:T(1,128)S(1)}, f32[2,1,2048]{2,1,0:T(1,128)S(1)}, u32[]{:S(2)}, u32[]{:S(2)}) %collective-permute-start.5) | collective-permute-done | bytes 16416 | tf_op jit(solution)/shard_map/ppermute | solution.py:45
  68.2 4.6 %collective-permute-start.6 = (f32[2,130,1]{2,1,0:T(8,128)S(1)}, f32[2,130,1]{2,1,0:T(8,128)S(1)}, u32[]{:S(2)}, u32[]{:S(2)}) collective-permute-start(f32[2,130,1]{2,1,0:T(8,128)S(1)} %get-tuple-element.518), channel_id=1, source_target_pairs={{0,1},{1,2},{2,3},{3,4},{4,5},{5,6},{6,7},{8,9},{9,10},{10,11},{11... | collective-permute-start | bytes 3128 | tf_op jit(solution)/shard_map/ppermute | solution.py:42
  74.4 5.1 %collective-permute-done.7 = f32[2,130,1]{2,1,0:T(8,128)S(1)} collective-permute-done((f32[2,130,1]{2,1,0:T(8,128)S(1)}, f32[2,130,1]{2,1,0:T(8,128)S(1)}, u32[]{:S(2)}, u32[]{:S(2)}) %collective-permute-start.7) | collective-permute-done | bytes 1072 | tf_op jit(solution)/shard_map/ppermute | solution.py:45
  79.5 4.1 %concatenate.67 = f32[2,130,2050]{2,1,0:T(8,128)} concatenate(f32[2,130,1]{2,1,0:T(8,128)S(1)} %collective-permute-done.6, f32[2,130,2048]{2,1,0:T(8,128)} %copy-done.10, f32[2,130,1]{2,1,0:T(8,128)S(1)} %collective-permute-done.7), dimensions={2} | concatenate | bytes 4264000 | tf_op jit(solution)/shard_map/concatenate | solution.py:46
  97.0 2.6 copy.11
  100.2 13.7 %all-gather.1 = f32[1024,1]{0,1:T(1,128)S(1)} all-gather(f32[128,1]{0,1:T(1,128)S(1)} %get-tuple-element.542), channel_id=3, replica_groups=mesh['rows'=4,'cols'=8] {'cols'}, dimensions={0}, use_global_device_ids=true | all-gather | bytes 4608 | tf_op jit(solution)/shard_map/all_gather | solution.py:25
  114.2 8.6 %all-gather = f32[1024,1]{0,1:T(1,128)S(1)} all-gather(f32[128,1]{0,1:T(1,128)S(1)} %get-tuple-element.537), channel_id=2, replica_groups=mesh['rows'=4,'cols'=8] {'cols'}, dimensions={0}, use_global_device_ids=true | all-gather | bytes 4608 | tf_op jit(solution)/shard_map/all_gather | solution.py:25
  122.8 15.5 %all-reduce.2 = (f32[128]{0:T(128)S(1)}, f32[128]{0:T(128)S(1)}) all-reduce(f32[128]{0:T(128)S(1)} %get-tuple-element.538, f32[128]{0:T(128)S(1)} %get-tuple-element.541), channel_id=1, replica_groups=mesh['rows'=4,'cols'=8] {'cols'}, use_global_device_ids=true, to_apply=%region_5.6 | all-reduce | flops 256 | bytes 2048 | tf_op jit(solution)/shard_map/psum | solution.py:194
  140.6 3.4 %collective-permute-start.8 = (f32[1,2048]{1,0:T(1,128)S(1)}, f32[1,2048]{1,0:T(1,128)S(1)}, u32[]{:S(2)}, u32[]{:S(2)}) collective-permute-start(f32[1,2048]{1,0:T(1,128)S(1)} %get-tuple-element.536), channel_id=1, source_target_pairs={{0,8},{8,16},{16,24},{1,9},{9,17},{17,25},{2,10},{10,18},{18,26},{... | collective-permute-start | bytes 24584 | tf_op jit(solution)/shard_map/ppermute | solution.py:42
  145.3 4.2 %collective-permute-done.9 = f32[1,2048]{1,0:T(1,128)S(1)} collective-permute-done((f32[1,2048]{1,0:T(1,128)S(1)}, f32[1,2048]{1,0:T(1,128)S(1)}, u32[]{:S(2)}, u32[]{:S(2)}) %collective-permute-start.9) | collective-permute-done | bytes 8224 | tf_op jit(solution)/shard_map/ppermute | solution.py:45
  150.9 3.7 %collective-permute-start.11 = (f32[130,1]{1,0:T(8,128)S(1)}, f32[130,1]{1,0:T(8,128)}, u32[]{:S(2)}, u32[]{:S(2)}) collective-permute-start(f32[130,1]{1,0:T(8,128)S(1)} %get-tuple-element.524), channel_id=1, source_target_pairs={{0,1},{1,2},{2,3},{3,4},{4,5},{5,6},{6,7},{8,9},{9,10},{10,11},{11... | collective-permute-start | bytes 1568 | tf_op jit(solution)/shard_map/ppermute | solution.py:42
  155.0 6.8 %fusion.34 = f32[128,2048]{1,0:T(8,128)S(1)} fusion(f32[128,2048]{1,0:T(8,128)S(1)} %fusion.55, f32[128,2048]{1,0:T(8,128)} %copy-done.3, f32[1,2048]{1,0:T(1,128)S(1)} %collective-permute-done.8, f32[1,2048]{1,0:T(1,128)S(1)} %collective-permute-done.9, f32[130,1]{1,0:T(8,128)} %collective-permute-done.11, f32[130,1]{1,0:T(8,128)S(1)} %collective-permute-done.10, ...), kind=kLoop, calls=%fused_computation.72 | loop fusion | flops 8126464 | bytes 9454608 | tf_op jit(solution)/shard_map/mul | solution.py:223
  174.8 11.0 %all-gather.2 = f32[1024,1]{0,1:T(1,128)S(1)} all-gather(f32[128,1]{0,1:T(1,128)S(1)} %get-tuple-element.531), channel_id=4, replica_groups=mesh['rows'=4,'cols'=8] {'cols'}, dimensions={0}, use_global_device_ids=true | all-gather | bytes 4608 | tf_op jit(solution)/shard_map/all_gather | solution.py:25
  185.8 8.7 %all-gather.3 = f32[1024,1]{0,1:T(1,128)S(1)} all-gather(f32[128,1]{0,1:T(1,128)S(1)} %get-tuple-element.533), channel_id=5, replica_groups=mesh['rows'=4,'cols'=8] {'cols'}, dimensions={0}, use_global_device_ids=true | all-gather | bytes 4608 | tf_op jit(solution)/shard_map/all_gather | solution.py:25
  194.7 15.1 %all-reduce.1 = (f32[128]{0:T(128)S(1)}, f32[128]{0:T(128)S(1)}) all-reduce(f32[128]{0:T(128)S(1)} %get-tuple-element.532, f32[128]{0:T(128)S(1)} %get-tuple-element.534), channel_id=1, replica_groups=mesh['rows'=4,'cols'=8] {'cols'}, use_global_device_ids=true, to_apply=%region_11.12 | all-reduce | flops 256 | bytes 2048 | tf_op jit(solution)/shard_map/psum | solution.py:194
  209.9 2.8 %multiply_add_fusion.2 = f32[128,2048]{1,0:T(8,128)S(1)} fusion(f32[128,2048]{1,0:T(8,128)} %copy-done.3, f32[128,2048]{1,0:T(8,128)} %copy-done.9, f32[128,2048]{1,0:T(8,128)} %copy.16, f32[128,2048]{1,0:T(8,128)} %copy.14, f32[128]{0:T(128)S(1)} %get-tuple-element.499, f32[128]{0:T(128)S(1)} %get-tuple-element.500, f32[128]{0:T(128)S(1)} %get-tuple-element.446, ...), kind=kLoop, calls=%fused_computation.144 | loop fusion | flops 3670016 | bytes 6326272 | tf_op jit(solution)/shard_map/add | solution.py:220
  212.7 2.8 collective-permute-start.12
  216.9 4.2 %collective-permute-done.13 = f32[1,2048]{1,0:T(1,128)S(1)} collective-permute-done((f32[1,2048]{1,0:T(1,128)S(1)}, f32[1,2048]{1,0:T(1,128)S(1)}, u32[]{:S(2)}, u32[]{:S(2)}) %collective-permute-start.13) | collective-permute-done | bytes 8224 | tf_op jit(solution)/shard_map/ppermute | solution.py:45
  222.5 3.7 %collective-permute-start.15 = (f32[130,1]{1,0:T(8,128)S(1)}, f32[130,1]{1,0:T(8,128)}, u32[]{:S(2)}, u32[]{:S(2)}) collective-permute-start(f32[130,1]{1,0:T(8,128)S(1)} %get-tuple-element.522), channel_id=1, source_target_pairs={{0,1},{1,2},{2,3},{3,4},{4,5},{5,6},{6,7},{8,9},{9,10},{10,11},{11... | collective-permute-start | bytes 1568 | tf_op jit(solution)/shard_map/ppermute | solution.py:42
  226.6 6.8 %fusion.20 = f32[128,2048]{1,0:T(8,128)S(1)} fusion(f32[128,2048]{1,0:T(8,128)S(1)} %fusion.55, f32[128,2048]{1,0:T(8,128)} %copy-done.4, f32[1,2048]{1,0:T(1,128)S(1)} %collective-permute-done.12, f32[1,2048]{1,0:T(1,128)S(1)} %collective-permute-done.13, f32[130,1]{1,0:T(8,128)} %collective-permute-done.15, f32[130,1]{1,0:T(8,128)S(1)} %collective-permute-done.14, ...), kind=kLoop, calls=%fused_computation.50 | loop fusion | flops 8126464 | bytes 9454608 | tf_op jit(solution)/shard_map/mul | solution.py:223
  246.4 11.0 %all-gather.4 = f32[1024,1]{0,1:T(1,128)S(1)} all-gather(f32[128,1]{0,1:T(1,128)S(1)} %get-tuple-element.525), channel_id=6, replica_groups=mesh['rows'=4,'cols'=8] {'cols'}, dimensions={0}, use_global_device_ids=true | all-gather | bytes 4608 | tf_op jit(solution)/shard_map/all_gather | solution.py:25
  257.4 8.7 %all-gather.5 = f32[1024,1]{0,1:T(1,128)S(1)} all-gather(f32[128,1]{0,1:T(1,128)S(1)} %get-tuple-element.527), channel_id=7, replica_groups=mesh['rows'=4,'cols'=8] {'cols'}, dimensions={0}, use_global_device_ids=true | all-gather | bytes 4608 | tf_op jit(solution)/shard_map/all_gather | solution.py:25
  266.3 14.9 %all-reduce = (f32[128]{0:T(128)S(1)}, f32[128]{0:T(128)S(1)}) all-reduce(f32[128]{0:T(128)S(1)} %get-tuple-element.526, f32[128]{0:T(128)S(1)} %get-tuple-element.528), channel_id=1, replica_groups=mesh['rows'=4,'cols'=8] {'cols'}, use_global_device_ids=true, to_apply=%region_17.18 | all-reduce | flops 256 | bytes 2048 | tf_op jit(solution)/shard_map/psum | solution.py:194
  281.2 3.2 %add_multiply_fusion = f32[128,2048]{1,0:T(8,128)} fusion(f32[128,2048]{1,0:T(8,128)S(1)} %copy-done.5, f32[128,2048]{1,0:T(8,128)S(1)} %copy-done.8, f32[128,2048]{1,0:T(8,128)} %copy.21, f32[128,2048]{1,0:T(8,128)} %copy.19, f32[128]{0:T(128)S(1)} %get-tuple-element.497, f32[128]{0:T(128)S(1)} %get-tuple-element.498, f32[128]{0:T(128)S(1)} %get-tuple-element.448, ...), kind=kLoop, calls=%fused_computation.141 | loop fusion | flops 3932160 | bytes 6326272 | tf_op jit(solution)/shard_map/mul | solution.py:224
  (152 shorter events, 70.8 us)
Async XLA Ops:
  0.6 13.8 %copy-start.11 = (f32[128,2048]{1,0:T(8,128)S(1)}, f32[128,2048]{1,0:T(8,128)}, u32[]{:S(2)}) copy-start(f32[128,2048]{1,0:T(8,128)} %param.18) | copy-start | bytes 3145732
  3.6 6.6 %collective-permute-start = (f32[6,1,2048]{2,1,0:T(1,128)S(1)}, f32[6,1,2048]{2,1,0:T(1,128)S(1)}, u32[]{:S(2)}, u32[]{:S(2)}) collective-permute-start(f32[6,1,2048]{2,1,0:T(1,128)S(1)} %get-tuple-element.514), channel_id=1, source_target_pairs={{0,8},{8,16},{16,24},{1,9},{9,17},{17,25},{2,10},{10,18},{18,26},{... | collective-permute-start | bytes 147464 | tf_op jit(solution)/shard_map/ppermute | solution.py:42
  8.5 6.0 %collective-permute-start.1 = (f32[6,1,2048]{2,1,0:T(1,128)S(1)}, f32[6,1,2048]{2,1,0:T(1,128)S(1)}, u32[]{:S(2)}, u32[]{:S(2)}) collective-permute-start(f32[6,1,2048]{2,1,0:T(1,128)S(1)} %get-tuple-element.513), channel_id=1, source_target_pairs={{8,0},{16,8},{24,16},{9,1},{17,9},{25,17},{10,2},{18,10},{26,18},{... | collective-permute-start | bytes 147464 | tf_op jit(solution)/shard_map/ppermute | solution.py:45
  9.8 14.9 %copy-start = (s32[128,2048]{1,0:T(8,128)S(1)}, s32[128,2048]{1,0:T(8,128)}, u32[]{:S(2)}) copy-start(s32[128,2048]{1,0:T(8,128)} %param.21) | copy-start | bytes 3145732
  17.3 2.8 copy-start.2
  20.3 5.5 %collective-permute-start.2 = (f32[6,130,1]{2,1,0:T(8,128)S(1)}, f32[6,130,1]{2,1,0:T(8,128)S(1)}, u32[]{:S(2)}, u32[]{:S(2)}) collective-permute-start(f32[6,130,1]{2,1,0:T(8,128)S(1)} %get-tuple-element.509), channel_id=1, source_target_pairs={{1,0},{2,1},{3,2},{4,3},{5,4},{6,5},{7,6},{9,8},{10,9},{11,10},{12... | collective-permute-start | bytes 9368 | tf_op jit(solution)/shard_map/ppermute | solution.py:45
  21.6 4.4 %collective-permute-start.3 = (f32[6,130,1]{2,1,0:T(8,128)S(1)}, f32[6,130,1]{2,1,0:T(8,128)S(1)}, u32[]{:S(2)}, u32[]{:S(2)}) collective-permute-start(f32[6,130,1]{2,1,0:T(8,128)S(1)} %get-tuple-element.510), channel_id=1, source_target_pairs={{0,1},{1,2},{2,3},{3,4},{4,5},{5,6},{6,7},{8,9},{9,10},{10,11},{11... | collective-permute-start | bytes 9368 | tf_op jit(solution)/shard_map/ppermute | solution.py:42
  36.4 2.9 %copy-start.1 = (f32[4,128,2048]{2,1,0:T(8,128)S(1)}, f32[4,128,2048]{2,1,0:T(8,128)}, u32[]{:S(2)}) copy-start(f32[4,128,2048]{2,1,0:T(8,128)} %param.17) | copy-start | bytes 12582916
  36.4 3.0 %copy-start.20 = (f32[6,130,1]{2,1,0:T(8,128)S(1)}, f32[6,130,1]{2,1,0:T(8,128)}, u32[]{:S(2)}) copy-start(f32[6,130,1]{2,1,0:T(8,128)} %copy-done.19) | copy-start | bytes 9364
  51.9 1.2 copy-start.17
  53.1 1.2 copy-start.18
  54.4 2.0 copy-start.6
  56.4 5.7 %collective-permute-start.4 = (f32[2,1,2048]{2,1,0:T(1,128)S(1)}, f32[2,1,2048]{2,1,0:T(1,128)S(1)}, u32[]{:S(2)}, u32[]{:S(2)}) collective-permute-start(f32[2,1,2048]{2,1,0:T(1,128)S(1)} %get-tuple-element.519), channel_id=1, source_target_pairs={{0,8},{8,16},{16,24},{1,9},{9,17},{17,25},{2,10},{10,18},{18,26},{... | collective-permute-start | bytes 49160 | tf_op jit(solution)/shard_map/ppermute | solution.py:42
  60.7 5.7 %collective-permute-start.5 = (f32[2,1,2048]{2,1,0:T(1,128)S(1)}, f32[2,1,2048]{2,1,0:T(1,128)S(1)}, u32[]{:S(2)}, u32[]{:S(2)}) collective-permute-start(f32[2,1,2048]{2,1,0:T(1,128)S(1)} %get-tuple-element.520), channel_id=1, source_target_pairs={{8,0},{16,8},{24,16},{9,1},{17,9},{25,17},{10,2},{18,10},{26,18},{... | collective-permute-start | bytes 49160 | tf_op jit(solution)/shard_map/ppermute | solution.py:45
  66.7 1.4 copy-start.10
  68.2 6.2 %collective-permute-start.6 = (f32[2,130,1]{2,1,0:T(8,128)S(1)}, f32[2,130,1]{2,1,0:T(8,128)S(1)}, u32[]{:S(2)}, u32[]{:S(2)}) collective-permute-start(f32[2,130,1]{2,1,0:T(8,128)S(1)} %get-tuple-element.518), channel_id=1, source_target_pairs={{0,1},{1,2},{2,3},{3,4},{4,5},{5,6},{6,7},{8,9},{9,10},{10,11},{11... | collective-permute-start | bytes 3128 | tf_op jit(solution)/shard_map/ppermute | solution.py:42
  72.8 6.7 %collective-permute-start.7 = (f32[2,130,1]{2,1,0:T(8,128)S(1)}, f32[2,130,1]{2,1,0:T(8,128)S(1)}, u32[]{:S(2)}, u32[]{:S(2)}) collective-permute-start(f32[2,130,1]{2,1,0:T(8,128)S(1)} %get-tuple-element.517), channel_id=1, source_target_pairs={{1,0},{2,1},{3,2},{4,3},{5,4},{6,5},{7,6},{9,8},{10,9},{11,10},{12... | collective-permute-start | bytes 3128 | tf_op jit(solution)/shard_map/ppermute | solution.py:45
  140.5 9.0 %copy-start.3 = (f32[128,2048]{1,0:T(8,128)}, f32[128,2048]{1,0:T(8,128)S(1)}, u32[]{:S(2)}) copy-start(f32[128,2048]{1,0:T(8,128)S(1)} %multiply_multiply_fusion) | copy-start | bytes 3145732
  140.6 4.8 %collective-permute-start.8 = (f32[1,2048]{1,0:T(1,128)S(1)}, f32[1,2048]{1,0:T(1,128)S(1)}, u32[]{:S(2)}, u32[]{:S(2)}) collective-permute-start(f32[1,2048]{1,0:T(1,128)S(1)} %get-tuple-element.536), channel_id=1, source_target_pairs={{0,8},{8,16},{16,24},{1,9},{9,17},{17,25},{2,10},{10,18},{18,26},{... | collective-permute-start | bytes 24584 | tf_op jit(solution)/shard_map/ppermute | solution.py:42
  144.0 5.5 %collective-permute-start.9 = (f32[1,2048]{1,0:T(1,128)S(1)}, f32[1,2048]{1,0:T(1,128)S(1)}, u32[]{:S(2)}, u32[]{:S(2)}) collective-permute-start(f32[1,2048]{1,0:T(1,128)S(1)} %get-tuple-element.535), channel_id=1, source_target_pairs={{8,0},{16,8},{24,16},{9,1},{17,9},{25,17},{10,2},{18,10},{26,18},{... | collective-permute-start | bytes 24584 | tf_op jit(solution)/shard_map/ppermute | solution.py:45
  149.6 5.0 %collective-permute-start.10 = (f32[130,1]{1,0:T(8,128)S(1)}, f32[130,1]{1,0:T(8,128)S(1)}, u32[]{:S(2)}, u32[]{:S(2)}) collective-permute-start(f32[130,1]{1,0:T(8,128)S(1)} %get-tuple-element.523), channel_id=1, source_target_pairs={{1,0},{2,1},{3,2},{4,3},{5,4},{6,5},{7,6},{9,8},{10,9},{11,10},{12... | collective-permute-start | bytes 1568 | tf_op jit(solution)/shard_map/ppermute | solution.py:45
  150.9 4.1 %collective-permute-start.11 = (f32[130,1]{1,0:T(8,128)S(1)}, f32[130,1]{1,0:T(8,128)}, u32[]{:S(2)}, u32[]{:S(2)}) collective-permute-start(f32[130,1]{1,0:T(8,128)S(1)} %get-tuple-element.524), channel_id=1, source_target_pairs={{0,1},{1,2},{2,3},{3,4},{4,5},{5,6},{6,7},{8,9},{9,10},{10,11},{11... | collective-permute-start | bytes 1568 | tf_op jit(solution)/shard_map/ppermute | solution.py:42
  161.8 1.1 copy-start.9
  212.7 8.4 %copy-start.4 = (f32[128,2048]{1,0:T(8,128)}, f32[128,2048]{1,0:T(8,128)S(1)}, u32[]{:S(2)}) copy-start(f32[128,2048]{1,0:T(8,128)S(1)} %multiply_add_fusion.2) | copy-start | bytes 3145732
  212.7 4.2 %collective-permute-start.12 = (f32[1,2048]{1,0:T(1,128)S(1)}, f32[1,2048]{1,0:T(1,128)S(1)}, u32[]{:S(2)}, u32[]{:S(2)}) collective-permute-start(f32[1,2048]{1,0:T(1,128)S(1)} %get-tuple-element.530), channel_id=1, source_target_pairs={{0,8},{8,16},{16,24},{1,9},{9,17},{17,25},{2,10},{10,18},{18,26},{... | collective-permute-start | bytes 24584 | tf_op jit(solution)/shard_map/ppermute | solution.py:42
  215.6 5.5 %collective-permute-start.13 = (f32[1,2048]{1,0:T(1,128)S(1)}, f32[1,2048]{1,0:T(1,128)S(1)}, u32[]{:S(2)}, u32[]{:S(2)}) collective-permute-start(f32[1,2048]{1,0:T(1,128)S(1)} %get-tuple-element.529), channel_id=1, source_target_pairs={{8,0},{16,8},{24,16},{9,1},{17,9},{25,17},{10,2},{18,10},{26,18},{... | collective-permute-start | bytes 24584 | tf_op jit(solution)/shard_map/ppermute | solution.py:45
  221.2 5.0 %collective-permute-start.14 = (f32[130,1]{1,0:T(8,128)S(1)}, f32[130,1]{1,0:T(8,128)S(1)}, u32[]{:S(2)}, u32[]{:S(2)}) collective-permute-start(f32[130,1]{1,0:T(8,128)S(1)} %get-tuple-element.521), channel_id=1, source_target_pairs={{1,0},{2,1},{3,2},{4,3},{5,4},{6,5},{7,6},{9,8},{10,9},{11,10},{12... | collective-permute-start | bytes 1568 | tf_op jit(solution)/shard_map/ppermute | solution.py:45
  222.5 4.1 %collective-permute-start.15 = (f32[130,1]{1,0:T(8,128)S(1)}, f32[130,1]{1,0:T(8,128)}, u32[]{:S(2)}, u32[]{:S(2)}) collective-permute-start(f32[130,1]{1,0:T(8,128)S(1)} %get-tuple-element.522), channel_id=1, source_target_pairs={{0,1},{1,2},{2,3},{3,4},{4,5},{5,6},{6,7},{8,9},{9,10},{10,11},{11... | collective-permute-start | bytes 1568 | tf_op jit(solution)/shard_map/ppermute | solution.py:42
  233.3 3.2 %copy-start.7 = (f32[128,2048]{1,0:T(8,128)}, f32[128,2048]{1,0:T(8,128)S(1)}, u32[]{:S(2)}) copy-start(f32[128,2048]{1,0:T(8,128)S(1)} %fusion.20) | copy-start | bytes 3145732
  236.8 44.5 %copy-start.5 = (f32[128,2048]{1,0:T(8,128)S(1)}, f32[128,2048]{1,0:T(8,128)}, u32[]{:S(2)}) copy-start(f32[128,2048]{1,0:T(8,128)} %copy-done.4) | copy-start | bytes 3145732
  236.8 44.5 %copy-start.8 = (f32[128,2048]{1,0:T(8,128)S(1)}, f32[128,2048]{1,0:T(8,128)}, u32[]{:S(2)}) copy-start(f32[128,2048]{1,0:T(8,128)} %copy-done.7) | copy-start | bytes 3145732
  242.9 1.0 copy-start.14
  (6 other events, 5.4 us)
where the time goes:
time: 286 us; the launch traced here: 284 us
  blocking collectives  107 us (37%)
  other arithmetic  53.8 us (19%)
  local copies, waits for them, and re-layouts  47.7 us (17%)
  starting transfers between devices  40.9 us (14%)
  waiting for transfers between devices  23.6 us (8%)
  matrix products  9.52 us (3%)
    all_gather x6, blocking collectives, carried_in(): gathered = jax.tree.map(lambda a: lax.all_gather(a, axis), part)  61.6 us
    psum x3, blocking collectives, line_solve(): lax.psum((local_starts * west_weight, local_ends * east_weight), 'cols')  45.5 us
    ppermute x8, starting transfers between devices, extended(): lax.ppermute(lax.slice_in_dim(block, block.shape[dim] - width, None, axis...  30.4 us
    ppermute x8, waiting for transfers between devices, extended(): lax.ppermute(lax.slice_in_dim(block, 0, width, axis=dim), axis, backward)  22 us
    mul x2, other arithmetic, per_device(): wet_cells * (forcing - operate(padded_level, padded_depth, stiffness))  13.5 us
    unnamed x44, local copies, waits for them, and re-layouts  13.4 us
    concatenate x2, local copies, waits for them, and re-layouts, extended(): block = jnp.concatenate([low, block, high], axis=dim)  13.2 us
    sub x1, other arithmetic, predict(): neighbour(velocity, rim_width, margin, 0, 1)  12 us
  transfers between devices with their start and end apart: 16, of which 10 were waited for; matrix products, arithmetic and copies ran while one was open for 0% of the time, Pallas kernels for 0%

commit v1 on v0

v1 whole, which is shorter than its diff:
```python
import functools
import math

import jax
import jax.numpy as jnp
import numpy as np
from jax import lax
from jax.experimental import pallas as pl
from jax.experimental.pallas import tpu as pltpu
from jax.sharding import PartitionSpec as P

ITERS = 3
REACH = 4096
BLOCK = 128
PAD = 8

coriolis_dt = 0.1
viscous_dt = 0.05
buoyant_dt = 0.2
top_share = 0.3
transport_dt = 0.5
cross_weight = 0.5
F32 = jnp.float32
MESH = pl.DeviceIdType.MESH
EXACT = lax.Precision.HIGHEST


def line_constants():
    base = 1.0 + 2.0 * cross_weight
    stiffness = base * REACH**2
    root = math.sqrt(base * base + 4.0 * base * stiffness)
    lag = (base + root) / (base + 2.0 * stiffness + root)
    gain = 1.0 / (base + 2.0 * stiffness * lag)
    return stiffness, lag, gain


def tables(length, count):
    _, lag, _ = line_constants()
    log = math.log1p(-lag)
    power = lambda n: np.exp(np.asarray(n, np.float64) * log)
    lane = np.arange(BLOCK)
    gap = lane[None, :] - lane[:, None]
    onward = np.where(gap >= 0, power(np.maximum(gap, 0)), 0.0)
    within = np.concatenate([onward, onward.T], axis=1)
    cell = np.arange(length)
    blocks = length // BLOCK
    gather = np.zeros((length, BLOCK))
    gather[:, 0] = gather[:, 3] = power(length - 1 - cell)
    gather[:, 1] = gather[:, 2] = power(cell)
    spread = np.zeros((BLOCK, BLOCK))
    for b in range(blocks):
        west, east = b * BLOCK, (b + 1) * BLOCK
        gather[:west, 8 + b] = power(west - 1 - cell[:west])
        gather[east:, 40 + b] = power(cell[east:] - east)
        spread[0, 8 + b] = spread[2, 8 + b] = power(west)
        spread[1, 40 + b] = spread[3, 40 + b] = power(length - east)
    q = float(power(length * count))
    hop = np.zeros((count, 8, BLOCK))
    for me in range(count):
        for k in range(count):
            p = (me - k) % count
            first, last = float(power(p * length)), float(power((count - 1 - p) * length))
            west_in, east_in = float(power(me * length)), float(power((count - 1 - me) * length))
            hop[me, 0, k] = west_in * q * last / (1 - q * q)
            hop[me, 2, k] = west_in * first / (1 - q * q)
            hop[me, 1, k] = east_in * q * first / (1 - q * q)
            hop[me, 3, k] = east_in * last / (1 - q * q)
            if p < me:
                hop[me, 0, k] += float(power((me - 1 - p) * length))
            if p > me:
                hop[me, 1, k] += float(power((p - me - 1) * length))
    edge = np.zeros((8, BLOCK))
    edge[0] = power(lane + 1)
    edge[1] = power(BLOCK - lane)
    return [np.asarray(a, np.float32) for a in (gather, within, spread, hop, edge)]


def transposed(rows8):
    return jnp.concatenate([rows8, jnp.zeros((BLOCK - 8, BLOCK), F32)], axis=0).T


def kernel(
    row_count, col_count, height, length,
    vel_hbm, gap_hbm, surf_hbm, depth_hbm, mask_hbm, gather_hbm,
    within, spread, hop, edge,
    pred_hbm, out_hbm,
    vel, gap, wd, mask, surf, gather, pred, fe, fn, ce, cw, cn, cs, res, on, bk, dl, lev, car,
    row_send, row_recv, col_send, col_recv, colw, cole, frow_send, frow_recv, fcol_send, fcol_recv,
    sum_send, sum_recv, drow_send, drow_recv,
    load_sem, out_sem, halo_ss, halo_rs, fh_ss, fh_rs, sum_ss, sum_rs, d_ss, d_rs,
):
    row = lax.axis_index("rows")
    col = lax.axis_index("cols")
    tiles = height // 8
    blocks = length // BLOCK
    stiffness, lag, gain = line_constants()
    decay = 1.0 - lag
    own = pl.ds(PAD, height)

    loads = [
        pltpu.make_async_copy(depth_hbm, wd.at[own], load_sem.at[0]),
        pltpu.make_async_copy(mask_hbm, mask, load_sem.at[1]),
        pltpu.make_async_copy(gap_hbm, gap.at[own], load_sem.at[2]),
        pltpu.make_async_copy(vel_hbm, vel.at[:, own], load_sem.at[3]),
        pltpu.make_async_copy(surf_hbm, surf, load_sem.at[4]),
        pltpu.make_async_copy(gather_hbm, gather, load_sem.at[5]),
    ]
    for load in loads:
        load.start()

    has_n, has_s = row > 0, row < row_count - 1
    has_w, has_e = col > 0, col < col_count - 1
    peers = [lax.rem(col + k, col_count) for k in range(1, col_count)]
    barrier = pltpu.get_barrier_semaphore()
    for peer in peers:
        pl.semaphore_signal(barrier, inc=1, device_id={"cols": peer}, device_id_type=MESH)

    @pl.when(has_n)
    def _():
        pl.semaphore_signal(barrier, inc=1, device_id={"rows": row - 1}, device_id_type=MESH)

    @pl.when(has_s)
    def _():
        pl.semaphore_signal(barrier, inc=1, device_id={"rows": row + 1}, device_id_type=MESH)

    neighbours = jnp.minimum(row, 1) + jnp.minimum(row_count - 1 - row, 1)
    pl.semaphore_wait(barrier, col_count - 1 + neighbours)

    def copies(send, recv, send_sem, recv_sem, axis, place):
        return [
            pltpu.make_async_remote_copy(
                src_ref=send.at[side], dst_ref=recv.at[1 - side],
                send_sem=send_sem.at[side], recv_sem=recv_sem.at[1 - side],
                device_id={axis: place + (2 * side - 1)}, device_id_type=MESH,
            )
            for side in range(2)
        ]

    def start(pair, low, high):
        pl.when(low)(pair[0].start)
        pl.when(high)(pair[1].start)

    def finish(pair, recv, low, high):
        for side, there in ((0, low), (1, high)):
            @pl.when(there)
            def _():
                pair[1 - side].wait_recv()
                pair[side].wait_send()

            @pl.when(jnp.logical_not(there))
            def _():
                recv[side] = jnp.zeros(recv.shape[1:], F32)

    row_halo = copies(row_send, row_recv, halo_ss.at[0], halo_rs.at[0], "rows", row)
    col_halo = copies(col_send, col_recv, halo_ss.at[1], halo_rs.at[1], "cols", col)
    frow_halo = copies(frow_send, frow_recv, fh_ss.at[0], fh_rs.at[0], "rows", row)
    fcol_halo = copies(fcol_send, fcol_recv, fh_ss.at[1], fh_rs.at[1], "cols", col)

    loads[0].wait()
    loads[1].wait()

    def wetten(t, carry):
        at = pl.ds(pl.multiple_of(PAD + 8 * t, 8), 8)
        wd[at, :] = wd[at, :] * mask[pl.ds(pl.multiple_of(8 * t, 8), 8), :].astype(F32)
        return carry

    lax.fori_loop(0, tiles, wetten, 0)
    loads[2].wait()
    loads[3].wait()

    fields = [vel.at[0], vel.at[1], vel.at[2], vel.at[3], gap, wd]
    lane = lax.broadcasted_iota(jnp.int32, (height, BLOCK), 1)
    west_pack = jnp.zeros((height, BLOCK), F32)
    east_pack = jnp.zeros((height, BLOCK), F32)
    for k, field in enumerate(fields):
        row_send[0, k : k + 1, :] = field[PAD : PAD + 1, :]
        row_send[1, k : k + 1, :] = field[PAD + height - 1 : PAD + height, :]
    start(row_halo, has_n, has_s)
    for k, field in enumerate(fields):
        low = field[PAD : PAD + height, 0:BLOCK]
        high = field[PAD : PAD + height, length - BLOCK : length]
        west_pack = jnp.where(lane == k, low if k == 0 else pltpu.roll(low, k, 1), west_pack)
        east_pack = jnp.where(lane == k, pltpu.roll(high, k + 1, 1), east_pack)
    col_send[0] = west_pack.T[0:8]
    col_send[1] = east_pack.T[0:8]
    start(col_halo, has_w, has_e)
    finish(row_halo, row_recv, has_n, has_s)
    finish(col_halo, col_recv, has_w, has_e)
    for k, field in enumerate(fields):
        field[PAD - 1 : PAD, :] = row_recv[0, k : k + 1, :]
        field[PAD + height : PAD + height + 1, :] = row_recv[1, k : k + 1, :]
    colw[...] = transposed(col_recv[0])
    cole[...] = transposed(col_recv[1])

    wide = lax.broadcasted_iota(jnp.int32, (8, length), 1)
    at_west, at_east = wide == 0, wide == length - 1

    def west_of(x, edge_column):
        return jnp.where(at_west, edge_column, pltpu.roll(x, 1, 1))

    def east_of(x, edge_column):
        return jnp.where(at_east, edge_column, pltpu.roll(x, length - 1, 1))

    def rows_of(t):
        return pl.ds(pl.multiple_of(8 * t, 8), 8)

    sub = lax.broadcasted_iota(jnp.int32, (8, length), 0)

    def three(ref, t):
        before = ref[rows_of(t), :]
        here = ref[rows_of(t + 1), :]
        after = ref[rows_of(t + 2), :]
        north = jnp.where(sub == 0, pltpu.roll(before, 1, 0), pltpu.roll(here, 1, 0))
        south = jnp.where(sub == 7, pltpu.roll(after, 7, 0), pltpu.roll(here, 7, 0))
        return here, north, south

    def momentum(t, carry):
        at = rows_of(t)
        depth_here = wd[rows_of(t + 1), :]
        wet = jnp.where(depth_here > 0.0, 1.0, 0.0)
        west_halo, east_halo = colw[at, :], cole[at, :]
        gap_here, gap_north, gap_south = three(gap, t)
        slope_east = 0.5 * (
            east_of(gap_here, east_halo[:, 4:5]) - west_of(gap_here, west_halo[:, 4:5])
        )
        slope_north = 0.5 * (gap_south - gap_north)
        for pair in range(2):
            parts = []
            for side in range(2):
                k = 2 * pair + side
                here, north, south = three(vel.at[k], t)
                lap = (
                    east_of(here, east_halo[:, k : k + 1])
                    + west_of(here, west_halo[:, k : k + 1])
                    + south + north - 4.0 * here
                )
                parts.append(here + viscous_dt * lap)
            u, v = vel[2 * pair, rows_of(t + 1), :], vel[2 * pair + 1, rows_of(t + 1), :]
            east = parts[0] + coriolis_dt * v
            north_part = parts[1] - coriolis_dt * u
            if pair == 1:
                east = east - buoyant_dt * slope_east
                north_part = north_part - buoyant_dt * slope_north
            pred[2 * pair, at, :] = wet * east
            pred[2 * pair + 1, at, :] = wet * north_part
        fe[at, :] = depth_here * (top_share * pred[0, at, :] + (1.0 - top_share) * pred[2, at, :])
        fn[rows_of(t + 1), :] = depth_here * (
            top_share * pred[1, at, :] + (1.0 - top_share) * pred[3, at, :]
        )
        return carry

    lax.fori_loop(0, tiles, momentum, 0)
    pred_out = pltpu.make_async_copy(pred, pred_hbm, out_sem.at[0])
    pred_out.start()

    frow_send[0] = fn[PAD : PAD + 1, :]
    frow_send[1] = fn[PAD + height - 1 : PAD + height, :]
    start(frow_halo, has_n, has_s)
    fcol_send[0] = fe[:, 0:BLOCK].T[0:8]
    fcol_send[1] = pltpu.roll(fe[:, length - BLOCK : length], 1, 1).T[0:8]
    start(fcol_halo, has_w, has_e)

    def conductances(t, carry):
        at = rows_of(t)
        here, north, south = three(wd, t)
        ce[at, :] = jnp.sqrt(here * east_of(here, cole[at, 5:6]))
        cw[at, :] = jnp.sqrt(here * west_of(here, colw[at, 5:6]))
        cn[at, :] = cross_weight * jnp.sqrt(here * north)
        cs[at, :] = cross_weight * jnp.sqrt(here * south)
        return carry

    lax.fori_loop(0, tiles, conductances, 0)
    finish(frow_halo, frow_recv, has_n, has_s)
    finish(fcol_halo, fcol_recv, has_w, has_e)
    fn[PAD - 1 : PAD, :] = frow_recv[0]
    fn[PAD + height : PAD + height + 1, :] = frow_recv[1]
    colw[...] = transposed(fcol_recv[0])
    cole[...] = transposed(fcol_recv[1])
    loads[4].wait()
    loads[5].wait()

    def force(t, carry):
        at = rows_of(t)
        east_flux = fe[at, :]
        _, north, south = three(fn, t)
        divergence = 0.5 * (
            east_of(east_flux, cole[at, 0:1]) - west_of(east_flux, colw[at, 0:1])
        ) + 0.5 * (south - north)
        wet = wd[rows_of(t + 1), :] > 0.0
        res[at, :] = jnp.where(wet, surf[at, :] - transport_dt * divergence, 0.0)
        return carry

    lax.fori_loop(0, tiles, force, 0)

    hop_here = hop[col]
    for it in range(ITERS):
        last = it + 1 == ITERS
        sums = jnp.dot(res[...], gather[...], precision=EXACT, preferred_element_type=F32)
        sum_send[it] = sums.T[0:8]
        sends = [
            pltpu.make_async_remote_copy(
                src_ref=sum_send.at[it], dst_ref=sum_recv.at[it, k],
                send_sem=sum_ss.at[it, k], recv_sem=sum_rs.at[it, k],
                device_id={"cols": peers[k - 1]}, device_id_type=MESH,
            )
            for k in range(1, col_count)
        ]
        for send in sends:
            send.start()

        for b in range(blocks):
            at = slice(b * BLOCK, (b + 1) * BLOCK)
            both = jnp.dot(res[:, at], within[...], precision=EXACT, preferred_element_type=F32)
            on[:, at] = both[:, :BLOCK]
            bk[:, at] = both[:, BLOCK:]

        entering = hop_here[:, 0:1] * sum_send[it]
        for k in range(1, col_count):
            sends[k - 1].wait_recv()
            entering = entering + hop_here[:, k : k + 1] * sum_recv[it, k]
        car[...] = sums + jnp.dot(
            transposed(entering), spread[...], precision=EXACT, preferred_element_type=F32
        )

        rising = jnp.broadcast_to(edge[0:1, :], (8, BLOCK))
        falling = jnp.broadcast_to(edge[1:2, :], (8, BLOCK))

        def solve(t, carry):
            at = rows_of(t)
            inner = rows_of(t + 1)
            enter = car[at, :]
            for b in range(blocks):
                cells = slice(b * BLOCK, (b + 1) * BLOCK)
                r = res[at, cells]
                o = on[at, cells] + rising * enter[:, 8 + b : 9 + b]
                w = bk[at, cells] + falling * enter[:, 40 + b : 41 + b]
                wet = wd[inner, cells] > 0.0
                d = jnp.where(wet, gain * (o + w - r), 0.0)
                if last:
                    lev[at, cells] = math.sqrt(REACH) * (lev[at, cells] + d)
                    continue
                if it == 0:
                    lev[at, cells] = d
                else:
                    lev[at, cells] = lev[at, cells] + d
                dl[inner, cells] = d
                flux_e = (w - r) * (1.0 / decay) - o
                flux_w = w - (o - r) * (1.0 / decay)
                scale = stiffness * gain * lag
                res[at, cells] = (
                    r - d + scale * (ce[at, cells] * flux_e - cw[at, cells] * flux_w)
                )
            return carry

        if last:
            lax.fori_loop(0, tiles, solve, 0)
            for send in sends:
                send.wait_send()
            break

        solve(0, 0)
        solve(tiles - 1, 0)
        drow_send[it, 0] = dl[PAD : PAD + 1, :]
        drow_send[it, 1] = dl[PAD + height - 1 : PAD + height, :]
        d_halo = copies(
            drow_send.at[it], drow_recv.at[it], d_ss.at[it], d_rs.at[it], "rows", row
        )
        start(d_halo, has_n, has_s)
        lax.fori_loop(1, tiles - 1, solve, 0)

        def cross(t, carry):
            at = rows_of(t)
            here, north, south = three(dl, t)
            value = res[at, :] - cn[at, :] * (here - north) - cs[at, :] * (here - south)
            res[at, :] = jnp.where(wd[rows_of(t + 1), :] > 0.0, value, 0.0)
            return carry

        lax.fori_loop(1, tiles - 1, cross, 0)
        finish(d_halo, drow_recv.at[it], has_n, has_s)
        dl[PAD - 1 : PAD, :] = drow_recv[it, 0]
        dl[PAD + height : PAD + height + 1, :] = drow_recv[it, 1]
        cross(0, 0)
        cross(tiles - 1, 0)
        for send in sends:
            send.wait_send()

    out = pltpu.make_async_copy(lev, out_hbm, out_sem.at[1])
    out.start()
    out.wait()
    pred_out.wait()


def per_device(row_count, col_count, velocity, layer_gap, surface, basin_depth, ocean_mask):
    height, length = surface.shape
    gather, within, spread, hop, edge = tables(length, col_count)
    padded = pltpu.VMEM((height + 2 * PAD, length), F32)
    plain = pltpu.VMEM((height, length), F32)
    tile = pltpu.VMEM((height, BLOCK), F32)
    dma = pltpu.SemaphoreType.DMA
    anywhere = pl.BlockSpec(memory_space=pl.ANY)
    vmem = pl.BlockSpec(memory_space=pltpu.VMEM)
    predicted, level = pl.pallas_call(
        functools.partial(kernel, row_count, col_count, height, length),
        out_shape=(
            jax.ShapeDtypeStruct(velocity.shape, F32),
            jax.ShapeDtypeStruct(surface.shape, F32),
        ),
        in_specs=[anywhere] * 6 + [vmem] * 4,
        out_specs=(anywhere, anywhere),
        scratch_shapes=[
            pltpu.VMEM((4, height + 2 * PAD, length), F32),
            padded, padded, pltpu.VMEM((height, length), jnp.int32), plain,
            pltpu.VMEM((length, BLOCK), F32),
            pltpu.VMEM((4, height, length), F32),
            plain, padded, plain, plain, plain, plain, plain, plain, plain, padded, plain, tile,
            pltpu.VMEM((2, 8, length), F32), pltpu.VMEM((2, 8, length), F32),
            pltpu.VMEM((2, 8, BLOCK), F32), pltpu.VMEM((2, 8, BLOCK), F32),
            tile, tile,
            pltpu.VMEM((2, 1, length), F32), pltpu.VMEM((2, 1, length), F32),
            pltpu.VMEM((2, 8, BLOCK), F32), pltpu.VMEM((2, 8, BLOCK), F32),
            pltpu.VMEM((ITERS, 8, BLOCK), F32), pltpu.VMEM((ITERS, col_count, 8, BLOCK), F32),
            pltpu.VMEM((ITERS, 2, 1, length), F32), pltpu.VMEM((ITERS, 2, 1, length), F32),
            dma((6,)), dma((2,)), dma((2, 2)), dma((2, 2)), dma((2, 2)), dma((2, 2)),
            dma((ITERS, col_count)), dma((ITERS, col_count)), dma((ITERS, 2)), dma((ITERS, 2)),
        ],
        compiler_params=pltpu.CompilerParams(
            collective_id=0, has_side_effects=True, vmem_limit_bytes=50 * 2**20
        ),
    )(velocity, layer_gap, surface, basin_depth, ocean_mask, gather, within, spread, hop, edge)
    return predicted, level


def solution(mesh):
    placed = (P(None, "rows", "cols"),) + (P("rows", "cols"),) * 4
    return jax.shard_map(
        functools.partial(per_device, mesh.shape["rows"], mesh.shape["cols"]),
        mesh=mesh,
        in_specs=placed,
        out_specs=(P(None, "rows", "cols"), P("rows", "cols")),
        check_vma=False,
    )
```

time: 286 us -> 57.8 us (0.20)
  blocking collectives: 107 us -> 0 us
  other arithmetic: 53.8 us -> 0 us
  Pallas kernels: 0 us -> 45.4 us
  starting transfers between devices: 40.9 us -> 0 us
  local copies, waits for them, and re-layouts: 47.7 us -> 11.3 us
  waiting for transfers between devices: 23.6 us -> 0 us
  matrix products: 9.52 us -> 0 us
    all_gather x6 -> x0, blocking collectives: 61.6 us -> none  [carried_in(): gathered = jax.tree.map(lambda a: lax.all_gather(a, axis), part)]
    psum x3 -> x0, blocking collectives: 45.5 us -> none  [line_solve(): lax.psum((local_starts * west_weight, local_ends * east_weight), 'cols')]
    pallas_call x0 -> x1, Pallas kernels: none -> 45.4 us  [per_device(): pl.pallas_call(functools.partial(kernel, row_count, col_count, height, le...]
    ppermute x16 -> x0, starting transfers between devices: 40.9 us -> none  [the longest x8 30.4 us: extended(): lax.ppermute(lax.slice_in_dim(block, block.shape[dim] - width, None, axis...]
    ppermute x16 -> x0, waiting for transfers between devices: 23.6 us -> none  [the longest x8 22 us: extended(): lax.ppermute(lax.slice_in_dim(block, 0, width, axis=dim), axis, backward)]
    mul x6 -> x0, other arithmetic: 21.7 us -> none  [the longest x2 13.5 us: per_device(): wet_cells * (forcing - operate(padded_level, padded_depth, stiffness))]
    reshape x6 -> x0, local copies, waits for them, and re-layouts: 15.3 us -> none  [the longest x3 7.67 us: sweeps(): backward_part.reshape(line_count, length)]
    concatenate x2 -> x0, local copies, waits for them, and re-layouts: 13.2 us -> none  [extended(): block = jnp.concatenate([low, block, high], axis=dim)]
  transfers between devices with their start and end apart: 16 -> 0, of which waited for: 10 -> 0; matrix products, arithmetic and copies ran while one was open for 0% -> 0% of each run, Pallas kernels for 0% -> 0%
where the time goes in v1:
time: 57.8 us; the launch traced here: 57.4 us
  Pallas kernels  45.4 us (79%)
  local copies, waits for them, and re-layouts  11.3 us (20%)
  between operations  0.65 us (1%)
    pallas_call x1, Pallas kernels, per_device(): pl.pallas_call(functools.partial(kernel, row_count, col_count, height, le...  45.4 us
    unnamed x14, local copies, waits for them, and re-layouts  11.3 us

profile of v1, /device:TPU:0, one launch (start us, length us, event | category | flops | bytes accessed | tf_op | source)
XLA Modules:
  0.0 57.4 jit_solution(10396956696089217199)
XLA Ops:
  0.6 0.0 copy-start
  0.6 1.2 %copy-done = f32[128,2048]{1,0:T(8,128)S(1)} copy-done((f32[128,2048]{1,0:T(8,128)S(1)}, f32[128,2048]{1,0:T(8,128)}, u32[]{:S(2)}) %copy-start) | copy-done | bytes 1048600
  1.9 0.0 copy-start.1
  1.9 1.2 %copy-done.1 = f32[128,2048]{1,0:T(8,128)S(1)} copy-done((f32[128,2048]{1,0:T(8,128)S(1)}, f32[128,2048]{1,0:T(8,128)}, u32[]{:S(2)}) %copy-start.1) | copy-done | bytes 1048600
  3.1 0.0 copy-start.2
  3.1 0.9 %copy-done.2 = f32[128,256]{1,0:T(8,128)S(1)} copy-done((f32[128,256]{1,0:T(8,128)S(1)}, f32[128,256]{1,0:T(8,128)}, u32[]{:S(2)}) %copy-start.2) | copy-done | bytes 131096
  4.0 0.0 copy-start.3
  4.0 0.8 %copy-done.3 = f32[128,128]{1,0:T(8,128)S(1)} copy-done((f32[128,128]{1,0:T(8,128)S(1)}, f32[128,128]{1,0:T(8,128)}, u32[]{:S(2)}) %copy-start.3) | copy-done | bytes 65560
  4.8 0.0 copy-start.4
  4.8 0.8 %copy-done.4 = f32[8,8,128]{2,1,0:T(8,128)S(1)} copy-done((f32[8,8,128]{2,1,0:T(8,128)S(1)}, f32[8,8,128]{2,1,0:T(8,128)}, u32[]{:S(2)}) %copy-start.4) | copy-done | bytes 32792
  5.6 0.0 copy-start.5
  5.6 0.7 %copy-done.5 = f32[8,128]{1,0:T(8,128)S(1)} copy-done((f32[8,128]{1,0:T(8,128)S(1)}, f32[8,128]{1,0:T(8,128)}, u32[]{:S(2)}) %copy-start.5) | copy-done | bytes 4120
  6.3 45.4 %shard_map.113 = (f32[4,128,2048]{2,1,0:T(8,128)}, f32[128,2048]{1,0:T(8,128)S(1)}) custom-call(f32[4,128,2048]{2,1,0:T(8,128)} %vel_hbm.1, f32[128,2048]{1,0:T(8,128)S(1)} %copy-done, f32[128,2048]{1,0:T(8,128)S(1)} %copy-done.1, f32[128,2048]{1,0:T(8,128)} %depth_hbm.1, s32[128,2048]{1,0:T(8,128)} %mask_hbm.1, f32[2048,128]{1,0:T(8,128)} %constant.10.clone.gather_hbm, ...), custom_call_target="tpu_custom_call" | custom-call | tf_op jit(solution)/shard_map/pallas_call | solution.py:402
  51.7 4.7 %copy.14 = f32[4,128,2048]{2,1,0:T(8,128)} copy(f32[4,128,2048]{2,1,0:T(8,128)} %get-tuple-element.4) | data formatting | bytes 8388608
  56.4 1.0 %copy.15 = f32[128,2048]{1,0:T(8,128)} copy(f32[128,2048]{1,0:T(8,128)S(1)} %get-tuple-element.5) | data formatting | bytes 2097152
Async XLA Ops:
  0.6 1.2 %copy-start = (f32[128,2048]{1,0:T(8,128)S(1)}, f32[128,2048]{1,0:T(8,128)}, u32[]{:S(2)}) copy-start(f32[128,2048]{1,0:T(8,128)} %gap_hbm.1) | copy-start | bytes 3145732
  1.9 1.2 %copy-start.1 = (f32[128,2048]{1,0:T(8,128)S(1)}, f32[128,2048]{1,0:T(8,128)}, u32[]{:S(2)}) copy-start(f32[128,2048]{1,0:T(8,128)} %surf_hbm.1) | copy-start | bytes 3145732
  3.1 0.9 %copy-start.2 = (f32[128,256]{1,0:T(8,128)S(1)}, f32[128,256]{1,0:T(8,128)}, u32[]{:S(2)}) copy-start(f32[128,256]{1,0:T(8,128)} %constant.11.clone.within) | copy-start | bytes 393220
  4.0 0.8 %copy-start.3 = (f32[128,128]{1,0:T(8,128)S(1)}, f32[128,128]{1,0:T(8,128)}, u32[]{:S(2)}) copy-start(f32[128,128]{1,0:T(8,128)} %constant.12.clone.spread) | copy-start | bytes 196612
  4.8 0.8 %copy-start.4 = (f32[8,8,128]{2,1,0:T(8,128)S(1)}, f32[8,8,128]{2,1,0:T(8,128)}, u32[]{:S(2)}) copy-start(f32[8,8,128]{2,1,0:T(8,128)} %constant.13.clone.hop) | copy-start | bytes 98308
  5.6 0.7 %copy-start.5 = (f32[8,128]{1,0:T(8,128)S(1)}, f32[8,128]{1,0:T(8,128)}, u32[]{:S(2)}) copy-start(f32[8,128]{1,0:T(8,128)} %constant.14.clone.edge) | copy-start | bytes 12292

commit v2 on v1

--- a/solution.py
+++ b/solution.py
@@ -72,7 +72,17 @@
     edge = np.zeros((8, BLOCK))
     edge[0] = power(lane + 1)
     edge[1] = power(BLOCK - lane)
-    return [np.asarray(a, np.float32) for a in (gather, within, spread, hop, edge)]
+    def split(a):
+        high = np.asarray(a, np.float32).astype(jnp.bfloat16)
+        return high, (a - high.astype(np.float64)).astype(np.float32).astype(jnp.bfloat16)
+
+    within_high, within_low = split(within)
+    halves = np.concatenate(
+        [np.concatenate(split(gather), axis=1), within_high, within_high, within_low],
+        axis=0,
+    )
+    exact = np.concatenate([spread, edge, hop.reshape(count * 8, BLOCK)]).astype(np.float32)
+    return halves.astype(np.float32), exact
 
 
 def transposed(rows8):
@@ -81,10 +91,9 @@
 
 def kernel(
     row_count, col_count, height, length,
-    vel_hbm, gap_hbm, surf_hbm, depth_hbm, mask_hbm, gather_hbm,
-    within, spread, hop, edge,
+    vel_hbm, gap_hbm, surf_hbm, depth_hbm, mask_hbm, halves_hbm, exact_hbm,
     pred_hbm, out_hbm,
-    vel, gap, wd, mask, surf, gather, pred, fe, fn, ce, cw, cn, cs, res, on, bk, dl, lev, car,
+    vel, gap, wd, mask, surf, wide_halves, halves, exact, vel_col, gap_col, depth_col, mask_col, split, pred, fe, fn, ce, cw, cn, cs, res, on, bk, dl, lev, car,
     row_send, row_recv, col_send, col_recv, colw, cole, frow_send, frow_recv, fcol_send, fcol_recv,
     sum_send, sum_recv, drow_send, drow_recv,
     load_sem, out_sem, halo_ss, halo_rs, fh_ss, fh_rs, sum_ss, sum_rs, d_ss, d_rs,
@@ -95,15 +104,33 @@
     blocks = length // BLOCK
     stiffness, lag, gain = line_constants()
     decay = 1.0 - lag
-    own = pl.ds(PAD, height)
-
+
+    middle = height - 16
+    sources = (
+        (depth_hbm, wd, depth_col, PAD, ()),
+        (mask_hbm, mask, mask_col, 0, ()),
+        (gap_hbm, gap, gap_col, PAD, ()),
+        (vel_hbm, vel, vel_col, PAD, (slice(None),)),
+    )
+    pairs = []
+    for start_row, size in ((0, 8), (height - 8, 8)):
+        for hbm, held, _, pad, lead in sources:
+            pairs.append((
+                hbm.at[lead + (pl.ds(start_row, size),)],
+                held.at[lead + (pl.ds(pad + start_row, size),)],
+            ))
+    for side, first in enumerate((0, length - BLOCK)):
+        for hbm, _, held, pad, lead in sources:
+            pairs.append((
+                hbm.at[lead + (slice(None), pl.ds(first, BLOCK))], held.at[side]
+            ))
+    for hbm, held, _, pad, lead in sources:
+        pairs.append((
+            hbm.at[lead + (pl.ds(8, middle),)], held.at[lead + (pl.ds(pad + 8, middle),)]
+        ))
+    pairs += [(surf_hbm, surf), (halves_hbm, wide_halves), (exact_hbm, exact)]
     loads = [
-        pltpu.make_async_copy(depth_hbm, wd.at[own], load_sem.at[0]),
-        pltpu.make_async_copy(mask_hbm, mask, load_sem.at[1]),
-        pltpu.make_async_copy(gap_hbm, gap.at[own], load_sem.at[2]),
-        pltpu.make_async_copy(vel_hbm, vel.at[:, own], load_sem.at[3]),
-        pltpu.make_async_copy(surf_hbm, surf, load_sem.at[4]),
-        pltpu.make_async_copy(gather_hbm, gather, load_sem.at[5]),
+        pltpu.make_async_copy(src, dst, load_sem.at[i]) for i, (src, dst) in enumerate(pairs)
     ]
     for load in loads:
         load.start()
@@ -156,8 +183,31 @@
     frow_halo = copies(frow_send, frow_recv, fh_ss.at[0], fh_rs.at[0], "rows", row)
     fcol_halo = copies(fcol_send, fcol_recv, fh_ss.at[1], fh_rs.at[1], "cols", col)
 
-    loads[0].wait()
-    loads[1].wait()
+    for load in loads[:8]:
+        load.wait()
+    for side, at in ((0, 0), (1, height - 1)):
+        for k in range(4):
+            row_send[side, k : k + 1, :] = vel[k, PAD + at : PAD + at + 1, :]
+        row_send[side, 4:5, :] = gap[PAD + at : PAD + at + 1, :]
+        row_send[side, 5:6, :] = (
+            wd[PAD + at : PAD + at + 1, :] * mask[at : at + 1, :].astype(F32)
+        )
+    start(row_halo, has_n, has_s)
+    for load in loads[8:16]:
+        load.wait()
+    lane = lax.broadcasted_iota(jnp.int32, (height, BLOCK), 1)
+    for side in range(2):
+        columns = [vel_col[side, k] for k in range(4)]
+        columns += [gap_col[side], depth_col[side] * mask_col[side].astype(F32)]
+        pack = jnp.zeros((height, BLOCK), F32)
+        for k, column in enumerate(columns):
+            pack = jnp.where(
+                lane == k, column if k + side == 0 else pltpu.roll(column, k + side, 1), pack
+            )
+        col_send[side] = pack.T[0:8]
+    start(col_halo, has_w, has_e)
+    for load in loads[16:20]:
+        load.wait()
 
     def wetten(t, carry):
         at = pl.ds(pl.multiple_of(PAD + 8 * t, 8), 8)
@@ -165,25 +215,7 @@
         return carry
 
     lax.fori_loop(0, tiles, wetten, 0)
-    loads[2].wait()
-    loads[3].wait()
-
     fields = [vel.at[0], vel.at[1], vel.at[2], vel.at[3], gap, wd]
-    lane = lax.broadcasted_iota(jnp.int32, (height, BLOCK), 1)
-    west_pack = jnp.zeros((height, BLOCK), F32)
-    east_pack = jnp.zeros((height, BLOCK), F32)
-    for k, field in enumerate(fields):
-        row_send[0, k : k + 1, :] = field[PAD : PAD + 1, :]
-        row_send[1, k : k + 1, :] = field[PAD + height - 1 : PAD + height, :]
-    start(row_halo, has_n, has_s)
-    for k, field in enumerate(fields):
-        low = field[PAD : PAD + height, 0:BLOCK]
-        high = field[PAD : PAD + height, length - BLOCK : length]
-        west_pack = jnp.where(lane == k, low if k == 0 else pltpu.roll(low, k, 1), west_pack)
-        east_pack = jnp.where(lane == k, pltpu.roll(high, k + 1, 1), east_pack)
-    col_send[0] = west_pack.T[0:8]
-    col_send[1] = east_pack.T[0:8]
-    start(col_halo, has_w, has_e)
     finish(row_halo, row_recv, has_n, has_s)
     finish(col_halo, col_recv, has_w, has_e)
     for k, field in enumerate(fields):
@@ -210,8 +242,8 @@
         before = ref[rows_of(t), :]
         here = ref[rows_of(t + 1), :]
         after = ref[rows_of(t + 2), :]
-        north = jnp.where(sub == 0, pltpu.roll(before, 1, 0), pltpu.roll(here, 1, 0))
-        south = jnp.where(sub == 7, pltpu.roll(after, 7, 0), pltpu.roll(here, 7, 0))
+        north = pltpu.roll(jnp.where(sub == 7, before, here), 1, 0)
+        south = pltpu.roll(jnp.where(sub == 0, after, here), 7, 0)
         return here, north, south
 
     def momentum(t, carry):
@@ -270,14 +302,21 @@
         return carry
 
     lax.fori_loop(0, tiles, conductances, 0)
+    for load in loads[20:]:
+        load.wait()
+
+    def narrow(t, carry):
+        at = pl.ds(pl.multiple_of(BLOCK * t, BLOCK), BLOCK)
+        halves[at, :] = wide_halves[at, :].astype(jnp.bfloat16)
+        return carry
+
+    lax.fori_loop(0, blocks + 3, narrow, 0)
     finish(frow_halo, frow_recv, has_n, has_s)
     finish(fcol_halo, fcol_recv, has_w, has_e)
     fn[PAD - 1 : PAD, :] = frow_recv[0]
     fn[PAD + height : PAD + height + 1, :] = frow_recv[1]
     colw[...] = transposed(fcol_recv[0])
     cole[...] = transposed(fcol_recv[1])
-    loads[4].wait()
-    loads[5].wait()
 
     def force(t, carry):
         at = rows_of(t)
@@ -292,10 +331,24 @@
 
     lax.fori_loop(0, tiles, force, 0)
 
-    hop_here = hop[col]
+    hop_here = exact[pl.ds(pl.multiple_of(BLOCK + 8 + 8 * col, 8), 8), :]
+    rising = jnp.broadcast_to(exact[BLOCK : BLOCK + 1, :], (8, BLOCK))
+    falling = jnp.broadcast_to(exact[BLOCK + 1 : BLOCK + 2, :], (8, BLOCK))
+    dot = functools.partial(jnp.dot, preferred_element_type=F32)
     for it in range(ITERS):
         last = it + 1 == ITERS
-        sums = jnp.dot(res[...], gather[...], precision=EXACT, preferred_element_type=F32)
+        for b in range(blocks):
+            at = slice(b * BLOCK, (b + 1) * BLOCK)
+            high = res[:, at].astype(jnp.bfloat16)
+            split[b, :, :BLOCK] = high
+            split[b, :, BLOCK:] = (res[:, at] - high.astype(F32)).astype(jnp.bfloat16)
+        total = jnp.zeros((height, 2 * BLOCK), F32)
+        small = jnp.zeros((height, BLOCK), F32)
+        for b in range(blocks):
+            weights = halves[b * BLOCK : (b + 1) * BLOCK, :]
+            total = total + dot(split[b, :, :BLOCK], weights)
+            small = small + dot(split[b, :, BLOCK:], weights[:, :BLOCK])
+        sums = total[:, :BLOCK] + total[:, BLOCK:] + small
         sum_send[it] = sums.T[0:8]
         sends = [
             pltpu.make_async_remote_copy(
@@ -310,7 +363,9 @@
 
         for b in range(blocks):
             at = slice(b * BLOCK, (b + 1) * BLOCK)
-            both = jnp.dot(res[:, at], within[...], precision=EXACT, preferred_element_type=F32)
+            both = dot(split[b], halves[length : length + 2 * BLOCK, :]) + dot(
+                split[b, :, :BLOCK], halves[length + 2 * BLOCK : length + 3 * BLOCK, :]
+            )
             on[:, at] = both[:, :BLOCK]
             bk[:, at] = both[:, BLOCK:]
 
@@ -319,11 +374,8 @@
             sends[k - 1].wait_recv()
             entering = entering + hop_here[:, k : k + 1] * sum_recv[it, k]
         car[...] = sums + jnp.dot(
-            transposed(entering), spread[...], precision=EXACT, preferred_element_type=F32
+            transposed(entering), exact[0:BLOCK, :], precision=EXACT, preferred_element_type=F32
         )
-
-        rising = jnp.broadcast_to(edge[0:1, :], (8, BLOCK))
-        falling = jnp.broadcast_to(edge[1:2, :], (8, BLOCK))
 
         def solve(t, carry):
             at = rows_of(t)
@@ -390,27 +442,38 @@
     pred_out.wait()
 
 
+def hand_on(pred_in, level_in, pred_out, level_out, sem):
+    moves = [pltpu.make_async_copy(pred_in.at[k], pred_out.at[k], sem.at[k]) for k in range(4)]
+    moves.append(pltpu.make_async_copy(level_in, level_out, sem.at[4]))
+    for move in moves:
+        move.start()
+    for move in moves:
+        move.wait()
+
+
 def per_device(row_count, col_count, velocity, layer_gap, surface, basin_depth, ocean_mask):
     height, length = surface.shape
-    gather, within, spread, hop, edge = tables(length, col_count)
+    halves, exact = tables(length, col_count)
     padded = pltpu.VMEM((height + 2 * PAD, length), F32)
     plain = pltpu.VMEM((height, length), F32)
     tile = pltpu.VMEM((height, BLOCK), F32)
     dma = pltpu.SemaphoreType.DMA
     anywhere = pl.BlockSpec(memory_space=pl.ANY)
-    vmem = pl.BlockSpec(memory_space=pltpu.VMEM)
     predicted, level = pl.pallas_call(
         functools.partial(kernel, row_count, col_count, height, length),
         out_shape=(
             jax.ShapeDtypeStruct(velocity.shape, F32),
             jax.ShapeDtypeStruct(surface.shape, F32),
         ),
-        in_specs=[anywhere] * 6 + [vmem] * 4,
+        in_specs=[anywhere] * 7,
         out_specs=(anywhere, anywhere),
         scratch_shapes=[
             pltpu.VMEM((4, height + 2 * PAD, length), F32),
             padded, padded, pltpu.VMEM((height, length), jnp.int32), plain,
-            pltpu.VMEM((length, BLOCK), F32),
+            pltpu.VMEM(halves.shape, F32), pltpu.VMEM(halves.shape, jnp.bfloat16), pltpu.VMEM(exact.shape, F32),
+            pltpu.VMEM((2, 4, height, BLOCK), F32), pltpu.VMEM((2, height, BLOCK), F32),
+            pltpu.VMEM((2, height, BLOCK), F32), pltpu.VMEM((2, height, BLOCK), jnp.int32),
+            pltpu.VMEM((length // BLOCK, height, 2 * BLOCK), jnp.bfloat16),
             pltpu.VMEM((4, height, length), F32),
             plain, padded, plain, plain, plain, plain, plain, plain, plain, padded, plain, tile,
             pltpu.VMEM((2, 8, length), F32), pltpu.VMEM((2, 8, length), F32),
@@ -420,14 +483,24 @@
             pltpu.VMEM((2, 8, BLOCK), F32), pltpu.VMEM((2, 8, BLOCK), F32),
             pltpu.VMEM((ITERS, 8, BLOCK), F32), pltpu.VMEM((ITERS, col_count, 8, BLOCK), F32),
             pltpu.VMEM((ITERS, 2, 1, length), F32), pltpu.VMEM((ITERS, 2, 1, length), F32),
-            dma((6,)), dma((2,)), dma((2, 2)), dma((2, 2)), dma((2, 2)), dma((2, 2)),
+            dma((23,)), dma((2,)), dma((2, 2)), dma((2, 2)), dma((2, 2)), dma((2, 2)),
             dma((ITERS, col_count)), dma((ITERS, col_count)), dma((ITERS, 2)), dma((ITERS, 2)),
         ],
         compiler_params=pltpu.CompilerParams(
-            collective_id=0, has_side_effects=True, vmem_limit_bytes=50 * 2**20
+            collective_id=0, has_side_effects=True, vmem_limit_bytes=60 * 2**20
         ),
-    )(velocity, layer_gap, surface, basin_depth, ocean_mask, gather, within, spread, hop, edge)
-    return predicted, level
+    )(velocity, layer_gap, surface, basin_depth, ocean_mask, halves, exact)
+    return pl.pallas_call(
+        hand_on,
+        out_shape=(
+            jax.ShapeDtypeStruct(velocity.shape, F32),
+            jax.ShapeDtypeStruct(surface.shape, F32),
+        ),
+        in_specs=[anywhere] * 2,
+        out_specs=(anywhere, anywhere),
+        scratch_shapes=[dma((5,))],
+        compiler_params=pltpu.CompilerParams(vmem_limit_bytes=60 * 2**20),
+    )(predicted, level)
 
 
 def solution(mesh):

time: 57.8 us -> 205 us (3.55)
  Pallas kernels: 45.4 us -> 204 us
  local copies, waits for them, and re-layouts: 11.3 us -> 0 us
    pallas_call x0 -> x1, Pallas kernels: none -> 160 us  [per_device(): pl.pallas_call(hand_on, out_shape=(jax.ShapeDtypeStruct(velocity.shape, F...]
    unnamed x14 -> x0, local copies, waits for them, and re-layouts: 11.3 us -> none
where the time goes in v2:
time: 205 us
  Pallas kernels  204 us (100%)
    pallas_call x1, Pallas kernels, per_device(): pl.pallas_call(hand_on, out_shape=(jax.ShapeDtypeStruct(velocity.shape, F...  160 us
    pallas_call x1, Pallas kernels, per_device(): pl.pallas_call(functools.partial(kernel, row_count, col_count, height, le...  44.5 us

profile of v2, /device:TPU:0, one launch (start us, length us, event | category | flops | bytes accessed | tf_op | source)
XLA Modules:
  0.0 205.1 jit_solution(6388469987974429402)
XLA Ops:
  0.6 44.5 %shard_map.86 = (f32[4,128,2048]{2,1,0:T(8,128)}, f32[128,2048]{1,0:T(8,128)}) custom-call(f32[4,128,2048]{2,1,0:T(8,128)} %vel_hbm.1, f32[128,2048]{1,0:T(8,128)} %gap_hbm.1, f32[128,2048]{1,0:T(8,128)} %surf_hbm.1, f32[128,2048]{1,0:T(8,128)} %depth_hbm.1, s32[128,2048]{1,0:T(8,128)} %mask_hbm.1, f32[2432,256]{1,0:T(8,128)} %constant.4.clone.halves_hbm, ...), custom_call_target="tpu_custom_call" | custom-call | tf_op jit(solution)/shard_map/pallas_call | solution.py:462
  45.1 160.0 %shard_map.87 = (f32[4,128,2048]{2,1,0:T(8,128)}, f32[128,2048]{1,0:T(8,128)}) custom-call(f32[4,128,2048]{2,1,0:T(8,128)} %get-tuple-element.4.pred_in, f32[128,2048]{1,0:T(8,128)} %get-tuple-element.5.level_in), custom_call_target="tpu_custom_call" | custom-call | tf_op jit(solution)/shard_map/pallas_call | solution.py:493

commit v3 on v2

--- a/solution.py
+++ b/solution.py
@@ -216,11 +216,7 @@
 
     lax.fori_loop(0, tiles, wetten, 0)
     fields = [vel.at[0], vel.at[1], vel.at[2], vel.at[3], gap, wd]
-    finish(row_halo, row_recv, has_n, has_s)
     finish(col_halo, col_recv, has_w, has_e)
-    for k, field in enumerate(fields):
-        field[PAD - 1 : PAD, :] = row_recv[0, k : k + 1, :]
-        field[PAD + height : PAD + height + 1, :] = row_recv[1, k : k + 1, :]
     colw[...] = transposed(col_recv[0])
     cole[...] = transposed(col_recv[1])
 
@@ -281,7 +277,13 @@
         )
         return carry
 
-    lax.fori_loop(0, tiles, momentum, 0)
+    lax.fori_loop(1, tiles - 1, momentum, 0)
+    finish(row_halo, row_recv, has_n, has_s)
+    for k, field in enumerate(fields):
+        field[PAD - 1 : PAD, :] = row_recv[0, k : k + 1, :]
+        field[PAD + height : PAD + height + 1, :] = row_recv[1, k : k + 1, :]
+    outer = lambda i, carry: momentum(i * (tiles - 1), carry)
+    lax.fori_loop(0, 2, outer, 0)
     pred_out = pltpu.make_async_copy(pred, pred_hbm, out_sem.at[0])
     pred_out.start()
 
@@ -442,13 +444,22 @@
     pred_out.wait()
 
 
-def hand_on(pred_in, level_in, pred_out, level_out, sem):
-    moves = [pltpu.make_async_copy(pred_in.at[k], pred_out.at[k], sem.at[k]) for k in range(4)]
-    moves.append(pltpu.make_async_copy(level_in, level_out, sem.at[4]))
-    for move in moves:
-        move.start()
-    for move in moves:
-        move.wait()
+def hand_on(pred_in, level_in, pred_out, level_out, held, in_sem, out_sem):
+    sources = [pred_in.at[k] for k in range(4)] + [level_in]
+    targets = [pred_out.at[k] for k in range(4)] + [level_out]
+    reads = [
+        pltpu.make_async_copy(src, held.at[k], in_sem.at[k]) for k, src in enumerate(sources)
+    ]
+    writes = [
+        pltpu.make_async_copy(held.at[k], dst, out_sem.at[k]) for k, dst in enumerate(targets)
+    ]
+    for read in reads:
+        read.start()
+    for read, write in zip(reads, writes):
+        read.wait()
+        write.start()
+    for write in writes:
+        write.wait()
 
 
 def per_device(row_count, col_count, velocity, layer_gap, surface, basin_depth, ocean_mask):
@@ -498,7 +509,7 @@
         ),
         in_specs=[anywhere] * 2,
         out_specs=(anywhere, anywhere),
-        scratch_shapes=[dma((5,))],
+        scratch_shapes=[pltpu.VMEM((5, height, length), F32), dma((5,)), dma((5,))],
         compiler_params=pltpu.CompilerParams(vmem_limit_bytes=60 * 2**20),
     )(predicted, level)
 

time: 205 us -> 47.8 us (0.23)
  Pallas kernels: 204 us -> 47 us
    pallas_call x1, Pallas kernels: 160 us -> 4.38 us  [per_device(): pl.pallas_call(hand_on, out_shape=(jax.ShapeDtypeStruct(velocity.shape, F...]
where the time goes in v3:
time: 47.8 us; the launch traced here: 47.6 us
  Pallas kernels  47 us (98%)
  between operations  0.64 us (1%)
    pallas_call x1, Pallas kernels, per_device(): pl.pallas_call(functools.partial(kernel, row_count, col_count, height, le...  42.6 us
    pallas_call x1, Pallas kernels, per_device(): pl.pallas_call(hand_on, out_shape=(jax.ShapeDtypeStruct(velocity.shape, F...  4.38 us

profile of v3, /device:TPU:0, one launch (start us, length us, event | category | flops | bytes accessed | tf_op | source)
XLA Modules:
  0.0 47.6 jit_solution(11422567333886716996)
XLA Ops:
  0.6 42.6 %shard_map.86 = (f32[4,128,2048]{2,1,0:T(8,128)}, f32[128,2048]{1,0:T(8,128)}) custom-call(f32[4,128,2048]{2,1,0:T(8,128)} %vel_hbm.1, f32[128,2048]{1,0:T(8,128)} %gap_hbm.1, f32[128,2048]{1,0:T(8,128)} %surf_hbm.1, f32[128,2048]{1,0:T(8,128)} %depth_hbm.1, s32[128,2048]{1,0:T(8,128)} %mask_hbm.1, f32[2432,256]{1,0:T(8,128)} %constant.4.clone.halves_hbm, ...), custom_call_target="tpu_custom_call" | custom-call | tf_op jit(solution)/shard_map/pallas_call | solution.py:473
  43.2 4.4 %shard_map.87 = (f32[4,128,2048]{2,1,0:T(8,128)}, f32[128,2048]{1,0:T(8,128)}) custom-call(f32[4,128,2048]{2,1,0:T(8,128)} %get-tuple-element.4.pred_in, f32[128,2048]{1,0:T(8,128)} %get-tuple-element.5.level_in), custom_call_target="tpu_custom_call" | custom-call | tf_op jit(solution)/shard_map/pallas_call | solution.py:504

commit v4 on v3

--- a/solution.py
+++ b/solution.py
@@ -445,19 +445,26 @@
 
 
 def hand_on(pred_in, level_in, pred_out, level_out, held, in_sem, out_sem):
-    sources = [pred_in.at[k] for k in range(4)] + [level_in]
-    targets = [pred_out.at[k] for k in range(4)] + [level_out]
+    half = level_in.shape[0] // 2
+    bands = [pl.ds(0, half), pl.ds(half, half)]
+    sources = [pred_in.at[k, band] for k in range(4) for band in bands]
+    sources += [level_in.at[band] for band in bands]
+    targets = [pred_out.at[k, band] for k in range(4) for band in bands]
+    targets += [level_out.at[band] for band in bands]
+    ahead = 3
     reads = [
         pltpu.make_async_copy(src, held.at[k], in_sem.at[k]) for k, src in enumerate(sources)
     ]
     writes = [
         pltpu.make_async_copy(held.at[k], dst, out_sem.at[k]) for k, dst in enumerate(targets)
     ]
-    for read in reads:
+    for read in reads[:ahead]:
         read.start()
-    for read, write in zip(reads, writes):
+    for k, (read, write) in enumerate(zip(reads, writes)):
         read.wait()
         write.start()
+        if k + ahead < len(reads):
+            reads[k + ahead].start()
     for write in writes:
         write.wait()
 
@@ -509,7 +516,7 @@
         ),
         in_specs=[anywhere] * 2,
         out_specs=(anywhere, anywhere),
-        scratch_shapes=[pltpu.VMEM((5, height, length), F32), dma((5,)), dma((5,))],
+        scratch_shapes=[pltpu.VMEM((10, height // 2, length), F32), dma((10,)), dma((10,))],
         compiler_params=pltpu.CompilerParams(vmem_limit_bytes=60 * 2**20),
     )(predicted, level)
 

time: 47.8 us -> 49.6 us (1.038)
  Pallas kernels: 47 us -> 48.7 us
    pallas_call x1, Pallas kernels: 4.38 us -> 6.1 us  [per_device(): pl.pallas_call(hand_on, out_shape=(jax.ShapeDtypeStruct(velocity.shape, F...]
where the time goes in v4:
time: 49.6 us; the launch traced here: 49.3 us
  Pallas kernels  48.7 us (98%)
  between operations  0.64 us (1%)
    pallas_call x1, Pallas kernels, per_device(): pl.pallas_call(functools.partial(kernel, row_count, col_count, height, le...  42.6 us
    pallas_call x1, Pallas kernels, per_device(): pl.pallas_call(hand_on, out_shape=(jax.ShapeDtypeStruct(velocity.shape, F...  6.1 us

profile of v4, /device:TPU:0, one launch (start us, length us, event | category | flops | bytes accessed | tf_op | source)
XLA Modules:
  0.0 49.3 jit_solution(17670394572928369785)
XLA Ops:
  0.6 42.6 %shard_map.86 = (f32[4,128,2048]{2,1,0:T(8,128)}, f32[128,2048]{1,0:T(8,128)}) custom-call(f32[4,128,2048]{2,1,0:T(8,128)} %vel_hbm.1, f32[128,2048]{1,0:T(8,128)} %gap_hbm.1, f32[128,2048]{1,0:T(8,128)} %surf_hbm.1, f32[128,2048]{1,0:T(8,128)} %depth_hbm.1, s32[128,2048]{1,0:T(8,128)} %mask_hbm.1, f32[2432,256]{1,0:T(8,128)} %constant.4.clone.halves_hbm, ...), custom_call_target="tpu_custom_call" | custom-call | tf_op jit(solution)/shard_map/pallas_call | solution.py:480
  43.2 6.1 %shard_map.87 = (f32[4,128,2048]{2,1,0:T(8,128)}, f32[128,2048]{1,0:T(8,128)}) custom-call(f32[4,128,2048]{2,1,0:T(8,128)} %get-tuple-element.4.pred_in, f32[128,2048]{1,0:T(8,128)} %get-tuple-element.5.level_in), custom_call_target="tpu_custom_call" | custom-call | tf_op jit(solution)/shard_map/pallas_call | solution.py:511
